TPU v7x, 512 devices: a whole 4x8x8 slice. The times are simulated.
512 devices in a mesh: pipe: 32 (over y, z_lo, core), tp: 16 (over x, z_hi).
Axes of the slice: x: 4, y: 8, z: 8 (z_hi: 4, z_lo: 2; z = z_hi * 2 + z_lo), core: 2. Of those that a mesh axis runs over, the one named last changes fastest.
Arguments:
- act_in: bfloat16 [32, 256, 12288], P('pipe', None, 'tp'), may hold values from -8 to 8
- grad_in: bfloat16 [32, 256, 12288], P('pipe', None, 'tp'), may hold values from -6 to 6
- held: bfloat16 [32, 256, 12288], P('pipe', None, 'tp'), may hold values from -8 to 8
- park: int32 [32], replicated, may hold values from 0 to 1, as said below
- gain_q: float32 [32, 12288], P('pipe', 'tp'), may hold values from 0.5 to 1.5
- gain_k: float32 [32, 12288], P('pipe', 'tp'), may hold values from 0.5 to 1.5
- gain_v: float32 [32, 12288], P('pipe', 'tp'), may hold values from 0.5 to 1.5
Outputs:
- act_out: bfloat16 [32, 256, 12288], P('pipe', None, 'tp')
- grad_out: bfloat16 [32, 256, 12288], P('pipe', None, 'tp')
- held_out: bfloat16 [32, 256, 12288], P('pipe', None, 'tp')
Inputs may be any that keep to these rules, and one draw needn't show every extreme that they name: park is 0 on sections 16 and higher; among the lower sections both values occur.
All inputs are finite; a program needn't handle non-finite values.
Results may differ from a plain program's by a relative error of at most 0.0042.
Values may be sent and summed in bfloat16 or wider, within the bound.
A program may use at most 64 MiB of HBM per device.

v0:
```python
import jax
import jax.numpy as jnp
from jax import lax
from jax.sharding import PartitionSpec as P

HD = 128
D = 12288


EPS = 1e-05


def from_behind(x, axis, by):
    devices = lax.axis_size(axis)
    pairs = [(i, i + by) for i in range(devices) if 0 <= i + by < devices]
    return lax.ppermute(x, axis, pairs)


def heads_of(field):
    return field.reshape(field.shape[0], -1, HD)


def project(xf, rate, gain_q, gain_k, gain_v):
    normed = xf * rate
    query = (normed * gain_q).astype(jnp.bfloat16)
    keys = (normed * gain_k).astype(jnp.bfloat16)
    values = (normed * gain_v).astype(jnp.bfloat16)
    return (query, keys, values)


def softmax_of(query, keys):
    raw = jnp.einsum(
        "shd,thd->hst", heads_of(query), heads_of(keys), preferred_element_type=jnp.float32
    ) * HD ** (-0.5)
    positions = lax.broadcasted_iota(jnp.int32, (raw.shape[1], raw.shape[2]), 0)
    columns = lax.broadcasted_iota(jnp.int32, (raw.shape[1], raw.shape[2]), 1)
    raw = jnp.where((positions >= columns)[None], raw, -jnp.inf)
    top = jnp.max(raw, axis=-1, keepdims=True)
    powers = jnp.exp(raw - top)
    return powers / jnp.sum(powers, axis=-1, keepdims=True)


def shards(act_in, grad_in, held, park, gain_q, gain_k, gain_v):
    gq = gain_q[0]
    gk = gain_k[0]
    gv = gain_v[0]
    sections = lax.axis_size("pipe")
    section = lax.axis_index("pipe")
    far_flag = jnp.take(park, sections - 1 - section)
    saved_rows = lax.all_to_all(
        held.reshape(sections, -1), "pipe", split_axis=0, concat_axis=0, tiled=True
    )
    saved = lax.all_to_all(
        saved_rows[::-1], "pipe", split_axis=0, concat_axis=0, tiled=True
    ).reshape(held.shape)
    far_rows = lax.all_to_all(
        act_in.reshape(sections, -1), "pipe", split_axis=0, concat_axis=0, tiled=True
    )
    far_input = lax.all_to_all(
        far_rows[::-1], "pipe", split_axis=0, concat_axis=0, tiled=True
    ).reshape(act_in.shape)
    held_out = jnp.where(far_flag == 1, far_input, held)
    xf = act_in[0].astype(jnp.float32)
    squares = lax.psum(jnp.sum(xf * xf, axis=-1), "tp")
    rate = lax.rsqrt(squares / D + EPS)[:, None]
    query, keys, values = project(xf, rate, gq, gk, gv)
    probs_b = softmax_of(query, keys).astype(jnp.bfloat16)
    mixed = jnp.einsum(
        "hst,thd->shd", probs_b, heads_of(values), preferred_element_type=jnp.float32
    )
    output = (xf + mixed.reshape(xf.shape)).astype(jnp.bfloat16)
    act_out = from_behind(output[None], "pipe", 1)
    sf = saved[0].astype(jnp.float32)
    saved_squares = lax.psum(jnp.sum(sf * sf, axis=-1), "tp")
    saved_rate = lax.rsqrt(saved_squares / D + EPS)[:, None]
    s_query, s_keys, s_values = project(sf, saved_rate, gq, gk, gv)
    probs = softmax_of(s_query, s_keys)
    s_probs_b = probs.astype(jnp.bfloat16)
    grad = grad_in[0]
    g_heads = heads_of(grad)
    dval = jnp.einsum("hst,shd->thd", s_probs_b, g_heads, preferred_element_type=jnp.float32)
    dprob = jnp.einsum(
        "shd,thd->hst", g_heads, heads_of(s_values), preferred_element_type=jnp.float32
    )
    delta = jnp.sum(probs * dprob, axis=-1, keepdims=True)
    dscore = (probs * (dprob - delta) * HD ** (-0.5)).astype(jnp.bfloat16)
    dquery = jnp.einsum(
        "hst,thd->shd", dscore, heads_of(s_keys), preferred_element_type=jnp.float32
    )
    dkeys = jnp.einsum(
        "hst,shd->thd", dscore, heads_of(s_query), preferred_element_type=jnp.float32
    )
    dnorm = (
        dquery.reshape(sf.shape) * gq + dkeys.reshape(sf.shape) * gk + dval.reshape(sf.shape) * gv
    )
    total = lax.psum(jnp.sum(dnorm * sf, axis=-1), "tp")[:, None] / D
    dinput = saved_rate * dnorm - sf * saved_rate * saved_rate * saved_rate * total
    back = (grad.astype(jnp.float32) + dinput).astype(jnp.bfloat16)
    grad_out = from_behind(back[None], "pipe", -1)
    return (act_out, grad_out, held_out)


def solution(mesh):
    in_specs = (
        P("pipe", None, "tp"),
        P("pipe", None, "tp"),
        P("pipe", None, "tp"),
        P(),
        P("pipe", "tp"),
        P("pipe", "tp"),
        P("pipe", "tp"),
    )
    out_specs = (P("pipe", None, "tp"), P("pipe", None, "tp"), P("pipe", None, "tp"))
    return jax.shard_map(shards, mesh=mesh, in_specs=in_specs, out_specs=out_specs, check_vma=False)
```

profile of v0, /device:TPU:1, one launch (start us, length us, event | category | flops | bytes accessed | tf_op | source)
XLA Modules:
  0.0 217.7 jit_solution(6784950351603033925)
XLA Ops:
  0.6 2.5 %all_to_all.38 = bf16[32,1,6144]{2,1,0:T(2,128)(2,1)S(1)} reshape(bf16[1,256,768]{2,1,0:T(8,128)(2,1)} %param.9) | data formatting | bytes 786432 | tf_op jit(solution)/shard_map/all_to_all | solution.py:50
  3.6 2.9 %reduce.14 = bf16[32,6144]{1,0:T(8,128)(2,1)S(1)} reduce(bf16[32,1,6144]{2,1,0:T(2,128)(2,1)S(1)} %all_to_all.38, bf16[]{:T(256)} %broadcast.236), dimensions={1}, to_apply=%all_to_all.38.reduce_sub_computation | reduce | bytes 786434 | tf_op jit(solution)/shard_map/all_to_all | solution.py:50
  6.6 1.0 reshape.420
  7.6 10.6 %all-to-all-start = ((bf16[32,2,3072]{2,1,0:T(2,128)(2,1)}), bf16[32,2,3072]{2,1,0:T(2,128)(2,1)S(1)}, u32[]{:S(2)}, u32[]{:S(2)}) async-start(bf16[32,2,3072]{2,1,0:T(2,128)(2,1)} %reshape.420), calls=%async_computation | async-start | bytes 786432 | tf_op jit(solution)/shard_map/all_to_all | solution.py:50
  18.4 3.0 %reduce.16 = bf16[32,6144]{1,0:T(8,128)(2,1)S(1)} reduce(bf16[32,1,6144]{2,1,0:T(2,128)(2,1)S(1)} %all_to_all.39, bf16[]{:T(256)} %broadcast.236), dimensions={1}, to_apply=%all_to_all.39.reduce_sub_computation | reduce | bytes 786434 | tf_op jit(solution)/shard_map/all_to_all | solution.py:56
  21.4 1.0 reshape.424
  22.4 9.6 %all-to-all-done = bf16[32,2,3072]{2,1,0:T(2,128)(2,1)S(1)} async-done(((bf16[32,2,3072]{2,1,0:T(2,128)(2,1)}), bf16[32,2,3072]{2,1,0:T(2,128)(2,1)S(1)}, u32[]{:S(2)}, u32[]{:S(2)}) %all-to-all-start) | async-done | bytes 393248 | tf_op jit(solution)/shard_map/all_to_all | solution.py:50
  32.0 5.2 %all-to-all-start.2 = ((bf16[32,2,3072]{2,1,0:T(2,128)(2,1)}), bf16[32,2,3072]{2,1,0:T(2,128)(2,1)S(1)}, u32[]{:S(2)}, u32[]{:S(2)}) async-start(bf16[32,2,3072]{2,1,0:T(2,128)(2,1)} %reshape.424), calls=%async_computation.2 | async-start | bytes 786432 | tf_op jit(solution)/shard_map/all_to_all | solution.py:56
  37.8 1.1 rev.6
  38.9 0.9 reduce.15
  39.8 1.0 reshape.422
  40.8 10.3 %all-to-all-done.2 = bf16[32,2,3072]{2,1,0:T(2,128)(2,1)S(1)} async-done(((bf16[32,2,3072]{2,1,0:T(2,128)(2,1)}), bf16[32,2,3072]{2,1,0:T(2,128)(2,1)S(1)}, u32[]{:S(2)}, u32[]{:S(2)}) %all-to-all-start.2) | async-done | bytes 393248 | tf_op jit(solution)/shard_map/all_to_all | solution.py:56
  51.1 5.2 %all-to-all-start.1 = ((bf16[32,2,3072]{2,1,0:T(2,128)(2,1)}), bf16[32,2,3072]{2,1,0:T(2,128)(2,1)S(1)}, u32[]{:S(2)}, u32[]{:S(2)}) async-start(bf16[32,2,3072]{2,1,0:T(2,128)(2,1)} %reshape.422), calls=%async_computation.1 | async-start | bytes 786432 | tf_op jit(solution)/shard_map/all_to_all | solution.py:53
  56.6 0.9 copy.74
  57.5 0.6 iota_compare_fusion
  58.1 0.7 multiply_reduce_fusion.1
  59.4 1.1 rev.7
  60.5 0.9 reduce.17
  61.4 1.0 reshape.426
  62.4 7.8 %all-to-all-done.1 = bf16[32,2,3072]{2,1,0:T(2,128)(2,1)S(1)} async-done(((bf16[32,2,3072]{2,1,0:T(2,128)(2,1)}), bf16[32,2,3072]{2,1,0:T(2,128)(2,1)S(1)}, u32[]{:S(2)}, u32[]{:S(2)}) %all-to-all-start.1) | async-done | bytes 393248 | tf_op jit(solution)/shard_map/all_to_all | solution.py:53
  70.2 5.8 %all-to-all-start.3 = ((bf16[32,2,3072]{2,1,0:T(2,128)(2,1)}), bf16[32,2,3072]{2,1,0:T(2,128)(2,1)}, u32[]{:S(2)}, u32[]{:S(2)}) async-start(bf16[32,2,3072]{2,1,0:T(2,128)(2,1)} %reshape.426), calls=%async_computation.3 | async-start | bytes 786432 | tf_op jit(solution)/shard_map/all_to_all | solution.py:59
  76.4 3.9 %multiply_reduce_fusion = (f32[32,6144]{1,0:T(8,128)}, f32[32,6144]{1,0:T(8,128)S(1)}) fusion(bf16[32,1,6144]{2,1,0:T(2,128)(2,1)S(1)} %reshape.423), kind=kLoop, calls=%fused_computation.32 | loop fusion | flops 393216 | bytes 1966080 | tf_op jit(solution)/shard_map/mul | solution.py:74
  80.3 1.4 reshape.398
  81.7 1.5 copy.71
  83.2 1.3 mul.248
  84.5 42.3 %psum.22 = f32[256]{0:T(256)S(1)} all-reduce(f32[256]{0:T(256)S(1)} %reduce_sum.56), channel_id=1, replica_groups=mesh['pipe'=32,'tp'=16] {'tp'}, use_global_device_ids=true, to_apply=%region_5.6 | all-reduce | flops 256 | bytes 2048 | tf_op jit(solution)/shard_map/psum | solution.py:74
  126.9 1.5 multiply_select_fusion
  128.4 1.4 fusion.35
  130.1 1.8 fusion.22
  131.9 4.4 %fusion.11 = f32[6,128,256]{2,1,0:T(8,128)} fusion(f32[6,256,256]{2,1,0:T(8,128)} %fusion.22, f32[256,6,128]{0,2,1:T(8,128)S(1)} %copy.71, f32[256]{0:T(256)S(1)} %add_rsqrt_fusion, f32[6,128]{1,0:T(8,128)S(1)} %bitcast.84, f32[6,256,256]{1,2,0:T(8,128)} %get-tuple-element.19, f32[6,256]{1,0:T(8,128)S(1)} %get-tuple-element.18), kind=kOutput, calls=%fused_computation.16 | convolution fusion | flops 104007424 | bytes 4728832 | tf_op jit(solution)/shard_map/hst,thd->shd/dot_general | solution.py:87
  136.3 4.4 %fusion.10 = f32[6,128,256]{2,1,0:T(8,128)} fusion(f32[6,256,256]{2,1,0:T(8,128)} %fusion.22, f32[256,6,128]{0,2,1:T(8,128)S(1)} %copy.71, f32[256]{0:T(256)S(1)} %add_rsqrt_fusion, f32[6,128]{1,0:T(8,128)S(1)} %bitcast.80, f32[6,256,256]{1,2,0:T(8,128)} %get-tuple-element.19, f32[6,256]{1,0:T(8,128)S(1)} %get-tuple-element.18), kind=kOutput, calls=%fused_computation.15 | convolution fusion | flops 104007424 | bytes 4728832 | tf_op jit(solution)/shard_map/hst,shd->thd/dot_general | solution.py:90
  140.8 4.5 %fusion.15 = (f32[256]{0:T(256)}, f32[6,256,128]{1,2,0:T(8,128)}) fusion(f32[256,6,128]{0,2,1:T(8,128)S(1)} %copy.71, f32[6,128,256]{2,1,0:T(8,128)} %fusion.10, f32[6,128,256]{2,1,0:T(8,128)} %fusion.11, f32[6,128]{1,0:T(8,128)S(1)} %bitcast.85, f32[6,128]{1,0:T(8,128)S(1)} %bitcast.81, f32[6,128]{1,0:T(8,128)S(1)} %bitcast.88, ...), kind=kOutput, calls=%fused_computation.21 | convolution fusion | flops 103220736 | bytes 5128192 | tf_op jit(solution)/shard_map/hst,shd->thd/dot_general | solution.py:81
  145.3 1.4 copy.82
  146.7 32.7 %all-reduce = (f32[256]{0:T(256)}, f32[256]{0:T(256)S(1)}) all-reduce(f32[256]{0:T(256)S(1)} %copy-done.7, f32[256]{0:T(256)S(1)} %copy-done.12), channel_id=1, replica_groups=mesh['pipe'=32,'tp'=16] {'tp'}, use_global_device_ids=true, to_apply=%region_1.2 | all-reduce | flops 512 | bytes 4096 | tf_op jit(solution)/shard_map/psum | solution.py:64
  179.3 0.6 broadcast_multiply_fusion
  179.9 1.4 copy.78
  181.3 2.3 %copy.80 = f32[1,256,768]{2,1,0:T(8,128)} copy(f32[1,256,768]{1,2,0:T(8,128)} %bitcast.75) | data formatting | bytes 1572864 | tf_op jit(solution)/shard_map/reshape | solution.py:94
  183.6 2.4 %add_convert_fusion = bf16[1,256,768]{2,1,0:T(8,128)(2,1)} fusion(f32[1,256,768]{2,1,0:T(8,128)S(1)} %reshape.399, f32[1,256,768]{2,1,0:T(8,128)S(1)} %copy.82, f32[1,256,768]{2,1,0:T(8,128)} %copy.80, f32[1,256,768]{2,1,0:T(8,128)S(1)} %copy.78, bf16[1,256,768]{2,1,0:T(8,128)(2,1)} %param.8, f32[256]{0:T(256)} %broadcast_multiply_fusion, ...), kind=kLoop, calls=%fused_computation.25 | loop fusion | flops 2752512 | bytes 3943424 | tf_op jit(solution)/shard_map/convert_element_type | solution.py:98
  186.0 16.5 %collective-permute-start.1 = (bf16[1,256,768]{2,1,0:T(8,128)(2,1)}, bf16[1,256,768]{2,1,0:T(8,128)(2,1)}, u32[]{:S(2)}, u32[]{:S(2)}) collective-permute-start(bf16[1,256,768]{2,1,0:T(8,128)(2,1)} %add_convert_fusion), channel_id=1, source_target_pairs={{16,0},{32,16},{48,32},{64,48},{80,64},{96,80},{112,96},{128,112},... | collective-permute-start | bytes 1179656 | tf_op jit(solution)/shard_map/ppermute | solution.py:16
  202.6 0.7 multiply_select_fusion.1
  203.6 0.5 fusion.21
  204.5 3.3 %collective-permute-start = (bf16[1,256,768]{2,1,0:T(8,128)(2,1)S(1)}, bf16[1,256,768]{2,1,0:T(8,128)(2,1)S(1)}, u32[]{:S(2)}, u32[]{:S(2)}) collective-permute-start(bf16[1,256,768]{2,1,0:T(8,128)(2,1)S(1)} %add_convert_fusion.1), channel_id=1, source_target_pairs={{0,16},{16,32},{32,48},{48,64},{64,80},{80,96},{96,112},{112,128},... | collective-permute-start | bytes 1179656 | tf_op jit(solution)/shard_map/ppermute | solution.py:16
  207.8 0.7 dynamic-slice.2
  209.1 2.8 %reshape.427 = bf16[32,1,6144]{2,1,0:T(2,128)(2,1)S(1)} reshape(bf16[32,2,3072]{2,1,0:T(2,128)(2,1)} %all-to-all-done.3) | data formatting | bytes 786432
  211.9 2.3 %reduce.11 = bf16[32,6144]{1,0:T(8,128)(2,1)S(1)} reduce(bf16[32,1,6144]{2,1,0:T(2,128)(2,1)S(1)} %reshape.427, bf16[]{:T(256)} %constant.79), dimensions={1}, to_apply=%all_to_all.37.reduce_sub_computation | reduce | bytes 786434 | tf_op jit(solution)/shard_map/all_to_all | solution.py:59
  214.4 0.8 broadcast_select_fusion
  215.2 0.7 copy.106
  216.0 1.8 copy.107
  (50 shorter events, 3.8 us)
Async XLA Ops:
  3.1 15.1 %copy-start.1 = (bf16[1,256,768]{2,1,0:T(8,128)(2,1)S(1)}, bf16[1,256,768]{2,1,0:T(8,128)(2,1)}, u32[]{:S(2)}) copy-start(bf16[1,256,768]{2,1,0:T(8,128)(2,1)} %param.7) | copy-start | bytes 1179652
  7.6 24.3 %all-to-all-start = ((bf16[32,2,3072]{2,1,0:T(2,128)(2,1)}), bf16[32,2,3072]{2,1,0:T(2,128)(2,1)S(1)}, u32[]{:S(2)}, u32[]{:S(2)}) async-start(bf16[32,2,3072]{2,1,0:T(2,128)(2,1)} %reshape.420), calls=%async_computation | async-start | bytes 786432 | tf_op jit(solution)/shard_map/all_to_all | solution.py:50
  32.0 19.1 %all-to-all-start.2 = ((bf16[32,2,3072]{2,1,0:T(2,128)(2,1)}), bf16[32,2,3072]{2,1,0:T(2,128)(2,1)S(1)}, u32[]{:S(2)}, u32[]{:S(2)}) async-start(bf16[32,2,3072]{2,1,0:T(2,128)(2,1)} %reshape.424), calls=%async_computation.2 | async-start | bytes 786432 | tf_op jit(solution)/shard_map/all_to_all | solution.py:56
  39.8 16.7 %copy-start.8 = (f32[1,768]{1,0:T(1,128)S(1)}, f32[1,768]{1,0:T(1,128)}, u32[]{:S(2)}) copy-start(f32[1,768]{1,0:T(1,128)} %param.11) | copy-start | bytes 9220
  39.8 16.7 %copy-start.9 = (f32[1,768]{1,0:T(1,128)S(1)}, f32[1,768]{1,0:T(1,128)}, u32[]{:S(2)}) copy-start(f32[1,768]{1,0:T(1,128)} %param.12) | copy-start | bytes 9220
  39.8 16.7 %copy-start.10 = (f32[1,768]{1,0:T(1,128)S(1)}, f32[1,768]{1,0:T(1,128)}, u32[]{:S(2)}) copy-start(f32[1,768]{1,0:T(1,128)} %param.13) | copy-start | bytes 9220
  39.8 16.7 %copy-start.2 = (bf16[1,256,768]{2,1,0:T(8,128)(2,1)S(1)}, bf16[1,256,768]{2,1,0:T(8,128)(2,1)}, u32[]{:S(2)}) copy-start(bf16[1,256,768]{2,1,0:T(8,128)(2,1)} %param.8) | copy-start | bytes 1179652
  51.1 19.1 %all-to-all-start.1 = ((bf16[32,2,3072]{2,1,0:T(2,128)(2,1)}), bf16[32,2,3072]{2,1,0:T(2,128)(2,1)S(1)}, u32[]{:S(2)}, u32[]{:S(2)}) async-start(bf16[32,2,3072]{2,1,0:T(2,128)(2,1)} %reshape.422), calls=%async_computation.1 | async-start | bytes 786432 | tf_op jit(solution)/shard_map/all_to_all | solution.py:53
  70.2 138.9 %all-to-all-start.3 = ((bf16[32,2,3072]{2,1,0:T(2,128)(2,1)}), bf16[32,2,3072]{2,1,0:T(2,128)(2,1)}, u32[]{:S(2)}, u32[]{:S(2)}) async-start(bf16[32,2,3072]{2,1,0:T(2,128)(2,1)} %reshape.426), calls=%async_computation.3 | async-start | bytes 786432 | tf_op jit(solution)/shard_map/all_to_all | solution.py:59
  128.4 1.7 copy-start
  128.4 1.7 copy-start.3
  130.1 6.2 %copy-start.6 = (f32[6,256]{1,0:T(8,128)}, f32[6,256]{1,0:T(8,128)S(1)}, u32[]{:S(2)}) copy-start(f32[6,256]{1,0:T(8,128)S(1)} %get-tuple-element.18) | copy-start | bytes 18436
  145.3 1.4 copy-start.7
  145.3 1.4 copy-start.12
  183.6 19.0 %copy-start.11 = (f32[256]{0:T(256)S(1)}, f32[256]{0:T(256)}, u32[]{:S(2)}) copy-start(f32[256]{0:T(256)} %get-tuple-element.16) | copy-start | bytes 3076
  183.6 19.0 %copy-start.5 = (pred[256,256]{0,1:T(8,128)(4,1)S(1)}, pred[256,256]{0,1:T(8,128)(4,1)}, u32[]{:S(2)}) copy-start(pred[256,256]{0,1:T(8,128)(4,1)} %iota_compare_fusion) | copy-start | bytes 196612
  186.0 29.2 %collective-permute-start.1 = (bf16[1,256,768]{2,1,0:T(8,128)(2,1)}, bf16[1,256,768]{2,1,0:T(8,128)(2,1)}, u32[]{:S(2)}, u32[]{:S(2)}) collective-permute-start(bf16[1,256,768]{2,1,0:T(8,128)(2,1)} %add_convert_fusion), channel_id=1, source_target_pairs={{16,0},{32,16},{48,32},{64,48},{80,64},{96,80},{112,96},{128,112},... | collective-permute-start | bytes 1179656 | tf_op jit(solution)/shard_map/ppermute | solution.py:16
  204.2 3.6 %copy-start.13 = (s32[32]{0:T(128)S(1)}, s32[32]{0:T(128)}, u32[]{:S(2)}) copy-start(s32[32]{0:T(128)} %param.10) | copy-start | bytes 388
  204.5 10.7 %collective-permute-start = (bf16[1,256,768]{2,1,0:T(8,128)(2,1)S(1)}, bf16[1,256,768]{2,1,0:T(8,128)(2,1)S(1)}, u32[]{:S(2)}, u32[]{:S(2)}) collective-permute-start(bf16[1,256,768]{2,1,0:T(8,128)(2,1)S(1)} %add_convert_fusion.1), channel_id=1, source_target_pairs={{0,16},{16,32},{32,48},{48,64},{64,80},{80,96},{96,112},{112,128},... | collective-permute-start | bytes 1179656 | tf_op jit(solution)/shard_map/ppermute | solution.py:16
  209.1 5.3 %copy-start.4 = (bf16[1,256,768]{2,1,0:T(8,128)(2,1)S(1)}, bf16[1,256,768]{2,1,0:T(8,128)(2,1)}, u32[]{:S(2)}) copy-start(bf16[1,256,768]{2,1,0:T(8,128)(2,1)} %param.9) | copy-start | bytes 1179652
where the time goes:
time: 219 us; the launch traced here: 218 us
  blocking collectives  75 us (34%)
  starting transfers between devices  46.6 us (21%)
  local copies, waits for them, and re-layouts  28 us (13%)
  waiting for transfers between devices  27.6 us (13%)
  other arithmetic  21 us (10%)
  matrix products  17.8 us (8%)
    psum x1, blocking collectives, shards(): saved_squares = lax.psum(jnp.sum(sf * sf, axis=-1), 'tp')  42.3 us
    psum x1, blocking collectives, shards(): squares = lax.psum(jnp.sum(xf * xf, axis=-1), 'tp')  32.7 us
    ppermute x2, starting transfers between devices, from_behind(): return lax.ppermute(x, axis, pairs)  19.8 us
    unnamed x41, local copies, waits for them, and re-layouts  12 us
    all_to_all x1, starting transfers between devices, shards(): lax.all_to_all(held.reshape(sections, -1), 'pipe', split_axis=0, concat_a...  10.6 us
    all_to_all x1, waiting for transfers between devices, shards(): lax.all_to_all(act_in.reshape(sections, -1), 'pipe', split_axis=0, concat...  10.3 us
    all_to_all x1, waiting for transfers between devices, shards(): lax.all_to_all(held.reshape(sections, -1), 'pipe', split_axis=0, concat_a...  9.58 us
    all_to_all x1, waiting for transfers between devices, shards(): lax.all_to_all(saved_rows[::-1], 'pipe', split_axis=0, concat_axis=0, til...  7.76 us
  transfers between devices with their start and end apart: 6, of which 3 were waited for; matrix products, arithmetic and copies ran while one was open for 26% of the time, Pallas kernels for 0%

commit v1 on v0

v1 whole, which is shorter than its diff:
```python
import jax
import jax.numpy as jnp
from jax import lax
from jax.experimental import pallas as pl
from jax.experimental.pallas import tpu as pltpu
from jax.sharding import PartitionSpec as P

HD = 128
SEQ = 256
EPS = 1e-05
MESH = pl.DeviceIdType.MESH
F32 = jnp.float32
BF16 = jnp.bfloat16
SCALE = HD ** (-0.5)


def nt(a, b):
    return lax.dot_general(a, b, (((1,), (1,)), ((), ())), preferred_element_type=F32)


def tn(a, b):
    return lax.dot_general(a, b, (((0,), (0,)), ((), ())), preferred_element_type=F32)


def nn(a, b):
    return lax.dot_general(a, b, (((1,), (0,)), ((), ())), preferred_element_type=F32)


def row_sums(field):
    ones = jnp.ones((8, HD), F32)
    sums = lax.dot_general(
        ones, field, (((1,), (1,)), ((), ())),
        precision=lax.Precision.HIGHEST, preferred_element_type=F32,
    )
    return sums[0:1, 0:128], sums[0:1, 128:256]


def as_column(row):
    return jnp.transpose(jnp.broadcast_to(row, (128, 128)))


def softmax_rows(raw, first_row):
    rows = lax.broadcasted_iota(jnp.int32, raw.shape, 0) + first_row
    columns = lax.broadcasted_iota(jnp.int32, raw.shape, 1)
    raw = jnp.where(rows >= columns, raw * SCALE, -jnp.inf)
    top = jnp.max(raw, axis=-1, keepdims=True)
    powers = jnp.exp(raw - top)
    return powers * (1.0 / jnp.sum(powers, axis=-1, keepdims=True))


def kernel(
    heads, sections, width,
    act, grad, held, gq, gk, gv,
    act_out, grad_out, far,
    xs, gs, hs, ss, ys, dns, rate_f, rate_s, total_b, tacc,
    msg1, gat1, msg2, gat2, rmsg, rget,
    load_x, load_g, load_h, held_send, held_recv, y_send, y_recv, b_send, b_recv,
    far_send, far_recv, s1, r1, s2, r2, rs, rr, zsem,
):
    section = lax.axis_index("pipe")
    me = lax.axis_index("tp")
    mirror = sections - 1 - section
    nxt = section + 1
    prv = section - 1
    half = sections // 2
    features = width * heads * HD
    low = section < half
    first = section == 0
    last = section == sections - 1

    def cols(h):
        return pl.ds(pl.multiple_of(h * HD, HD), HD)

    def load(h, src, dst, sem):
        return pltpu.make_async_copy(src.at[0, :, cols(h)], dst.at[h], sem.at[h])

    def start_loads(h, c):
        load(h, act, xs, load_x).start()
        load(h, grad, gs, load_g).start()
        return c

    hload = pltpu.make_async_copy(held.at[0], hs, load_h)
    lax.fori_loop(0, heads, start_loads, 0)
    hload.start()

    barrier = pltpu.get_barrier_semaphore()

    def greet(p, c):
        pl.semaphore_signal(
            barrier, inc=1, device_id=(section, lax.rem(me + p, width)), device_id_type=MESH
        )
        return c

    pl.semaphore_signal(barrier, inc=1, device_id=(mirror, me), device_id_type=MESH)

    @pl.when(jnp.logical_not(last))
    def _():
        pl.semaphore_signal(barrier, inc=1, device_id=(nxt, me), device_id_type=MESH)

    @pl.when(jnp.logical_not(first))
    def _():
        pl.semaphore_signal(barrier, inc=1, device_id=(prv, me), device_id_type=MESH)

    lax.fori_loop(1, width, greet, 0)
    edge = jnp.where(jnp.logical_or(first, last), 1, 0)
    pl.semaphore_wait(barrier, width + 2 - edge)

    def held_copy(h):
        return pltpu.make_async_remote_copy(
            src_ref=held.at[0, :, cols(h)], dst_ref=ss.at[h],
            send_sem=held_send.at[h], recv_sem=held_recv.at[h],
            device_id=(mirror, me), device_id_type=MESH,
        )

    def start_held(h, c):
        held_copy(h).start()
        return c

    lax.fori_loop(0, heads, start_held, 0)

    def wait_loads(h, c):
        load(h, act, xs, load_x).wait()
        return c

    lax.fori_loop(0, heads, wait_loads, 0)

    def x_squares(h, acc):
        v = xs[h].astype(F32)
        return acc + v * v

    sq_x = lax.fori_loop(0, heads, x_squares, jnp.zeros((SEQ, HD), F32))
    hload.wait()

    def h_squares(h, acc):
        v = hs[:, cols(h)].astype(F32)
        return acc + v * v

    sq_h = lax.fori_loop(0, heads, h_squares, jnp.zeros((SEQ, HD), F32))
    a0, a1 = row_sums(sq_x)
    b0, b1 = row_sums(sq_h)
    parts = jnp.concatenate([a0, a1, b0, b1, jnp.zeros((4, 128), F32)], axis=0)
    msg1[...] = parts
    gat1[pl.ds(me, 1)] = parts[None]

    def exchange(msg, gat, ssem, rsem):
        def copy(p):
            return pltpu.make_async_remote_copy(
                src_ref=msg, dst_ref=gat.at[me],
                send_sem=ssem.at[p], recv_sem=rsem.at[p],
                device_id=(section, lax.rem(me + p, width)), device_id_type=MESH,
            )

        def start(p, c):
            copy(p).start()
            return c

        def wait(p, c):
            copy(p).wait()
            return c

        lax.fori_loop(1, width, start, 0)
        lax.fori_loop(1, width, wait, 0)
        return jnp.sum(gat[...], axis=0)

    sums = exchange(msg1, gat1, s1, r1)
    rates = lax.rsqrt(sums / features + EPS)
    rmsg[...] = rates
    rate_copy = pltpu.make_async_remote_copy(
        src_ref=rmsg, dst_ref=rget, send_sem=rs, recv_sem=rr,
        device_id=(mirror, me), device_id_type=MESH,
    )
    rate_copy.start()
    rate_f[pl.ds(0, 128)] = as_column(rates[0:1])
    rate_f[pl.ds(128, 128)] = as_column(rates[1:2])

    def project(xf, rate, h):
        normed = xf * rate
        return (
            (normed * gq[:, cols(h)]).astype(BF16),
            (normed * gk[:, cols(h)]).astype(BF16),
            (normed * gv[:, cols(h)]).astype(BF16),
        )

    def y_copy(h):
        return pltpu.make_async_remote_copy(
            src_ref=ys.at[h], dst_ref=act_out.at[0, :, cols(h)],
            send_sem=y_send.at[h], recv_sem=y_recv.at[h],
            device_id=(jnp.minimum(nxt, sections - 1), me), device_id_type=MESH,
        )

    def forward(h, c):
        xf = xs[h].astype(F32)
        q, k, v = project(xf, rate_f[...], h)
        p0 = softmax_rows(nt(q[0:128], k[0:128]), 0).astype(BF16)
        p1 = softmax_rows(nt(q[128:256], k), 128).astype(BF16)
        ys[h, pl.ds(0, 128)] = (xf[0:128] + nn(p0, v[0:128])).astype(BF16)
        ys[h, pl.ds(128, 128)] = (xf[128:256] + nn(p1, v)).astype(BF16)

        @pl.when(jnp.logical_not(last))
        def _():
            y_copy(h).start()

        return c

    lax.fori_loop(0, heads, forward, 0)

    rate_copy.wait()
    got = rget[...]
    rate_s[pl.ds(0, 128)] = as_column(got[2:3])
    rate_s[pl.ds(128, 128)] = as_column(got[3:4])
    tacc[...] = jnp.zeros((SEQ, HD), F32)

    def act_copy(h):
        return pltpu.make_async_remote_copy(
            src_ref=act.at[0, :, cols(h)], dst_ref=far.at[0, :, cols(h)],
            send_sem=far_send.at[h], recv_sem=far_recv.at[h],
            device_id=(mirror, me), device_id_type=MESH,
        )

    def backward(h, c):
        load(h, grad, gs, load_g).wait()
        held_copy(h).wait()

        @pl.when(low)
        def _():
            act_copy(h).start()

        xf = ss[h].astype(F32)
        q, k, v = project(xf, rate_s[...], h)
        g = gs[h]
        p0 = softmax_rows(nt(q[0:128], k[0:128]), 0)
        p1 = softmax_rows(nt(q[128:256], k), 128)
        d0 = nt(g[0:128], v[0:128])
        d1 = nt(g[128:256], v)

        def dscore(probs, dprob):
            delta = jnp.sum(probs * dprob, axis=-1, keepdims=True)
            return (probs * (dprob - delta) * SCALE).astype(BF16)

        e0 = dscore(p0, d0)
        e1 = dscore(p1, d1)
        dval = tn(p1.astype(BF16), g[128:256])
        dkey = tn(e1, q[128:256])
        dval0 = dval[0:128] + tn(p0.astype(BF16), g[0:128])
        dkey0 = dkey[0:128] + tn(e0, q[0:128])
        g_q, g_k, g_v = gq[:, cols(h)], gk[:, cols(h)], gv[:, cols(h)]
        dn0 = nn(e0, k[0:128]) * g_q + dkey0 * g_k + dval0 * g_v
        dn1 = nn(e1, k) * g_q + dkey[128:256] * g_k + dval[128:256] * g_v
        dns[h, pl.ds(0, 128)] = dn0
        dns[h, pl.ds(128, 128)] = dn1
        tacc[pl.ds(0, 128)] += dn0 * xf[0:128]
        tacc[pl.ds(128, 128)] += dn1 * xf[128:256]
        return c

    lax.fori_loop(0, heads, backward, 0)

    t0, t1 = row_sums(tacc[...])
    parts2 = jnp.concatenate([t0, t1, jnp.zeros((6, 128), F32)], axis=0)
    msg2[...] = parts2
    gat2[pl.ds(me, 1)] = parts2[None]
    totals = exchange(msg2, gat2, s2, r2) / features
    total_b[pl.ds(0, 128)] = as_column(totals[0:1])
    total_b[pl.ds(128, 128)] = as_column(totals[1:2])
    rate = rate_s[...]
    total_b[...] = total_b[...] * (rate * rate * rate)

    def b_copy(h):
        return pltpu.make_async_remote_copy(
            src_ref=gs.at[h], dst_ref=grad_out.at[0, :, cols(h)],
            send_sem=b_send.at[h], recv_sem=b_recv.at[h],
            device_id=(jnp.maximum(prv, 0), me), device_id_type=MESH,
        )

    def finish(h, c):
        dx = rate_s[...] * dns[h] - ss[h].astype(F32) * total_b[...]
        gs[h] = (gs[h].astype(F32) + dx).astype(BF16)

        @pl.when(jnp.logical_not(first))
        def _():
            b_copy(h).start()

        return c

    lax.fori_loop(0, heads, finish, 0)

    @pl.when(jnp.logical_or(first, last))
    def _():
        hs[...] = jnp.zeros(hs.shape, BF16)

    @pl.when(first)
    def _():
        copy = pltpu.make_async_copy(hs, act_out.at[0], zsem)
        copy.start()
        copy.wait()

    @pl.when(last)
    def _():
        copy = pltpu.make_async_copy(hs, grad_out.at[0], zsem)
        copy.start()
        copy.wait()

    def drain(h, c):
        @pl.when(jnp.logical_not(last))
        def _():
            y_copy(h).wait_send()
            b_copy(h).wait_recv()

        @pl.when(jnp.logical_not(first))
        def _():
            y_copy(h).wait_recv()
            b_copy(h).wait_send()

        @pl.when(low)
        def _():
            act_copy(h).wait_send()

        @pl.when(jnp.logical_not(low))
        def _():
            act_copy(h).wait_recv()

        return c

    lax.fori_loop(0, heads, drain, 0)


def solution(mesh):
    sections, width = mesh.shape["pipe"], mesh.shape["tp"]

    def shards(act_in, grad_in, held, park, gain_q, gain_k, gain_v):
        heads = act_in.shape[2] // HD
        block = jax.ShapeDtypeStruct(act_in.shape, BF16)
        hbm = pl.BlockSpec(memory_space=pl.ANY)
        vmem = pl.BlockSpec(memory_space=pltpu.VMEM)
        dma = pltpu.SemaphoreType.DMA

        def body(*refs):
            kernel(heads, sections, width, *refs)

        act_out, grad_out, far = pl.pallas_call(
            body,
            out_shape=(block, block, block),
            in_specs=[hbm, hbm, hbm, vmem, vmem, vmem],
            out_specs=(hbm, hbm, hbm),
            scratch_shapes=[
                pltpu.VMEM((heads, SEQ, HD), BF16),
                pltpu.VMEM((heads, SEQ, HD), BF16),
                pltpu.VMEM((SEQ, heads * HD), BF16),
                pltpu.VMEM((heads, SEQ, HD), BF16),
                pltpu.VMEM((heads, SEQ, HD), BF16),
                pltpu.VMEM((heads, SEQ, HD), F32),
                pltpu.VMEM((SEQ, HD), F32),
                pltpu.VMEM((SEQ, HD), F32),
                pltpu.VMEM((SEQ, HD), F32),
                pltpu.VMEM((SEQ, HD), F32),
                pltpu.VMEM((8, 128), F32),
                pltpu.VMEM((width, 8, 128), F32),
                pltpu.VMEM((8, 128), F32),
                pltpu.VMEM((width, 8, 128), F32),
                pltpu.VMEM((8, 128), F32),
                pltpu.VMEM((8, 128), F32),
                dma((heads,)), dma((heads,)), dma,
                dma((heads,)), dma((heads,)), dma((heads,)), dma((heads,)),
                dma((heads,)), dma((heads,)), dma((heads,)), dma((heads,)),
                dma((width,)), dma((width,)), dma((width,)), dma((width,)),
                dma, dma, dma,
            ],
            compiler_params=pltpu.CompilerParams(
                collective_id=0, has_side_effects=True, vmem_limit_bytes=24 * 1024 * 1024
            ),
            name="relay_tick",
        )(act_in, grad_in, held, gain_q, gain_k, gain_v)
        section = lax.axis_index("pipe")
        flag = jnp.take(park, sections - 1 - section)
        held_out = jnp.where(flag == 1, far, held)
        return act_out, grad_out, held_out

    wide = P("pipe", None, "tp")
    gain = P("pipe", "tp")
    return jax.shard_map(
        shards,
        mesh=mesh,
        in_specs=(wide, wide, wide, P(), gain, gain, gain),
        out_specs=(wide, wide, wide),
        check_vma=False,
    )
```

time: 219 us -> 69.5 us (0.32)
  the two profiles are of different devices: /device:TPU:1 before, /device:TPU:351 now
where the time goes in v1:
time: 69.5 us; the launch traced here: 69.2 us
  Pallas kernels  61.3 us (88%)
  local copies, waits for them, and re-layouts  5.7 us (8%)
  between operations  1.37 us (2%)
  other arithmetic  0.81 us (1%)
    pallas_call x1, Pallas kernels, shards(): pl.pallas_call(body, out_shape=(block, block, block), in_specs=[hbm, hbm,...  61.3 us
    unnamed x16, local copies, waits for them, and re-layouts  5.12 us

profile of v1, /device:TPU:351, one launch (start us, length us, event | category | flops | bytes accessed | tf_op | source)
XLA Modules:
  0.0 69.2 jit_solution(2268109693006859877)
XLA Ops:
  0.6 0.0 copy-start.6
  0.6 0.0 copy-start.5
  0.7 0.6 copy-done.6
  1.3 0.0 copy-start.4
  1.3 0.6 dynamic-slice.2
  1.9 0.0 copy-start.3
  2.5 0.0 copy-done.5
  2.6 0.0 copy-done.4
  2.6 0.0 copy-done.3
  2.6 0.0 copy-start
  2.6 1.0 %copy-done = bf16[1,256,768]{2,1,0:T(8,128)(2,1)S(1)} copy-done((bf16[1,256,768]{2,1,0:T(8,128)(2,1)S(1)}, bf16[1,256,768]{2,1,0:T(8,128)(2,1)}, u32[]{:S(2)}) %copy-start) | copy-done | bytes 393240
  3.6 0.0 copy-start.1
  3.6 1.0 %copy-done.1 = bf16[1,256,768]{2,1,0:T(8,128)(2,1)S(1)} copy-done((bf16[1,256,768]{2,1,0:T(8,128)(2,1)S(1)}, bf16[1,256,768]{2,1,0:T(8,128)(2,1)}, u32[]{:S(2)}) %copy-start.1) | copy-done | bytes 393240
  4.6 0.0 copy-start.2
  4.6 1.0 %copy-done.2 = bf16[1,256,768]{2,1,0:T(8,128)(2,1)S(1)} copy-done((bf16[1,256,768]{2,1,0:T(8,128)(2,1)S(1)}, bf16[1,256,768]{2,1,0:T(8,128)(2,1)}, u32[]{:S(2)}) %copy-start.2) | copy-done | bytes 393240
  5.6 61.3 %relay_tick.1 = (bf16[1,256,768]{2,1,0:T(8,128)(2,1)S(1)}, bf16[1,256,768]{2,1,0:T(8,128)(2,1)S(1)}, bf16[1,256,768]{2,1,0:T(8,128)(2,1)S(1)}) custom-call(bf16[1,256,768]{2,1,0:T(8,128)(2,1)S(1)} %copy-done.1, bf16[1,256,768]{2,1,0:T(8,128)(2,1)S(1)} %copy-done.2, bf16[1,256,768]{2,1,0:T(8,128)(2,1)S(1)} %copy-done, f32[1,768]{1,0:T(1,128)S(1)} %copy-done.3, ...), custom_call_target="tpu_custom_call" | custom-call | tf_op jit(solution)/shard_map/relay_tick/pallas_call | solution.py:339
  66.9 0.8 %broadcast_select_fusion = bf16[1,256,768]{2,1,0:T(8,128)(2,1)} fusion(bf16[1,256,768]{2,1,0:T(8,128)(2,1)S(1)} %get-tuple-element.8, bf16[1,256,768]{2,1,0:T(8,128)(2,1)S(1)} %copy-done, pred[]{:T(512)} %bitcast.1), kind=kLoop, calls=%fused_computation | loop fusion | flops 196608 | bytes 1179649 | tf_op jit(solution)/shard_map/jit(_where)/select_n | solution.py:374
  67.7 0.7 %copy.12 = bf16[1,256,768]{2,1,0:T(8,128)(2,1)} copy(bf16[1,256,768]{2,1,0:T(8,128)(2,1)S(1)} %get-tuple-element.23) | data formatting | bytes 786432
  68.5 0.7 %copy.13 = bf16[1,256,768]{2,1,0:T(8,128)(2,1)} copy(bf16[1,256,768]{2,1,0:T(8,128)(2,1)S(1)} %get-tuple-element.24) | data formatting | bytes 786432
Async XLA Ops:
  0.6 0.7 copy-start.6
  0.6 1.9 %copy-start.5 = (f32[1,768]{1,0:T(1,128)S(1)}, f32[1,768]{1,0:T(1,128)}, u32[]{:S(2)}) copy-start(f32[1,768]{1,0:T(1,128)} %refs_5_.1) | copy-start | bytes 9220
  1.3 1.3 %copy-start.4 = (f32[1,768]{1,0:T(1,128)S(1)}, f32[1,768]{1,0:T(1,128)}, u32[]{:S(2)}) copy-start(f32[1,768]{1,0:T(1,128)} %refs_4_.1) | copy-start | bytes 9220
  1.9 0.7 %copy-start.3 = (f32[1,768]{1,0:T(1,128)S(1)}, f32[1,768]{1,0:T(1,128)}, u32[]{:S(2)}) copy-start(f32[1,768]{1,0:T(1,128)} %refs_3_.1) | copy-start | bytes 9220
  2.6 1.0 %copy-start = (bf16[1,256,768]{2,1,0:T(8,128)(2,1)S(1)}, bf16[1,256,768]{2,1,0:T(8,128)(2,1)}, u32[]{:S(2)}) copy-start(bf16[1,256,768]{2,1,0:T(8,128)(2,1)} %refs_2_.1) | copy-start | bytes 1179652
  3.6 1.0 %copy-start.1 = (bf16[1,256,768]{2,1,0:T(8,128)(2,1)S(1)}, bf16[1,256,768]{2,1,0:T(8,128)(2,1)}, u32[]{:S(2)}) copy-start(bf16[1,256,768]{2,1,0:T(8,128)(2,1)} %refs_0_.1) | copy-start | bytes 1179652
  4.6 1.0 %copy-start.2 = (bf16[1,256,768]{2,1,0:T(8,128)(2,1)S(1)}, bf16[1,256,768]{2,1,0:T(8,128)(2,1)}, u32[]{:S(2)}) copy-start(bf16[1,256,768]{2,1,0:T(8,128)(2,1)} %refs_1_.1) | copy-start | bytes 1179652

commit v2 on v1

v2 whole, which is shorter than its diff:
```python
import jax
import jax.numpy as jnp
from jax import lax
from jax.experimental import pallas as pl
from jax.experimental.pallas import tpu as pltpu
from jax.sharding import PartitionSpec as P

HD = 128
SEQ = 256
EPS = 1e-05
MESH = pl.DeviceIdType.MESH
F32 = jnp.float32
BF16 = jnp.bfloat16
SCALE = HD ** (-0.5)
FIRST = 2


def nt(a, b):
    return lax.dot_general(a, b, (((1,), (1,)), ((), ())), preferred_element_type=F32)


def tn(a, b):
    return lax.dot_general(a, b, (((0,), (0,)), ((), ())), preferred_element_type=F32)


def nn(a, b):
    return lax.dot_general(a, b, (((1,), (0,)), ((), ())), preferred_element_type=F32)


def row_sums(field):
    ones = jnp.ones((8, HD), F32)
    sums = lax.dot_general(
        ones, field, (((1,), (1,)), ((), ())),
        precision=lax.Precision.HIGHEST, preferred_element_type=F32,
    )
    return sums[0:1, 0:128], sums[0:1, 128:256]


def as_column(row):
    return jnp.transpose(jnp.broadcast_to(row, (128, 128)))


def softmax_rows(raw, first_row):
    rows = lax.broadcasted_iota(jnp.int32, raw.shape, 0) + first_row
    columns = lax.broadcasted_iota(jnp.int32, raw.shape, 1)
    raw = jnp.where(rows >= columns, raw * SCALE, -jnp.inf)
    top = jnp.max(raw, axis=-1, keepdims=True)
    powers = jnp.exp(raw - top)
    return powers * (1.0 / jnp.sum(powers, axis=-1, keepdims=True))


def kernel(
    heads, sections, width,
    act, grad, held, park, gq_in, gk_in, gv_in,
    act_out, grad_out, held_out,
    xs, gs, hs, ss, ys, xn, zs, far, gq, gk, gv, flags,
    rate_f, rate_s, tacc,
    msg1, gat1, msg3, gat3, hsum, hsum_got, esum, esum_got, rate_e, rate_e_got, bo, ho,
    load_x, load_g, load_h, load_p, load_w,
    held_send, held_recv, y_send, y_recv, b_send, b_recv, far_send, far_recv,
    s1, r1, s3, r3, hs_send, hs_recv, es, er, rs, rr, ho_sem, zero_sem,
    hello, near,
):
    section = lax.axis_index("pipe")
    me = lax.axis_index("tp")
    mirror = sections - 1 - section
    nxt = jnp.minimum(section + 1, sections - 1)
    prv = jnp.maximum(section - 1, 0)
    features = width * heads * HD
    odd = lax.rem(section, 2) == 1
    even = lax.rem(section, 2) == 0
    first = section == 0
    last = section == sections - 1
    half = sections // 2
    low = section < half
    inner = jnp.logical_and(section >= half // 4, section < half - half // 4)
    depth = lax.rem(me, 4)
    act_first = jnp.logical_and(low, jnp.logical_not(inner))
    act_mid = jnp.logical_and(inner, depth < 1)
    act_aft = jnp.logical_and(inner, jnp.logical_and(depth >= 1, depth < 1))
    act_later = jnp.logical_and(inner, jnp.logical_and(depth >= 1, depth >= 1))

    def cols(h):
        return pl.ds(pl.multiple_of(h * HD, HD), HD)

    def each_head(f):
        def step(h, c):
            f(h)
            return c

        lax.fori_loop(0, heads, step, 0)

    def each_peer(start, f):
        def step(p, c):
            f(p)
            return c

        lax.fori_loop(start, width, step, 0)

    def remote(src, dst, send, recv, device):
        return pltpu.make_async_remote_copy(
            src_ref=src, dst_ref=dst, send_sem=send, recv_sem=recv,
            device_id=device, device_id_type=MESH,
        )

    def signal(sem, device):
        pl.semaphore_signal(sem, inc=1, device_id=device, device_id_type=MESH)

    def held_copy(h):
        return remote(held.at[0, :, cols(h)], ss.at[h], held_send.at[h], held_recv.at[h], (mirror, me))

    def act_copy(h):
        return remote(act.at[0, :, cols(h)], far.at[h], far_send.at[h], far_recv.at[h], (mirror, me))

    def y_copy(h):
        return remote(ys.at[h], act_out.at[0, :, cols(h)], y_send.at[h], y_recv.at[h], (nxt, me))

    def b_copy(h):
        return remote(bo.at[h], grad_out.at[0, :, cols(h)], b_send.at[h], b_recv.at[h], (prv, me))

    def sum_copy(msg, gat, send, recv, p):
        return remote(msg, gat.at[me], send.at[p], recv.at[p], (section, lax.rem(me + p, width)))

    def total_copy(p):
        return remote(msg3, gat3.at[me], s3.at[p], r3.at[p], (section, lax.rem(me + p, width)))

    hsum_copy = remote(hsum, hsum_got, hs_send, hs_recv, (mirror, me))
    esum_copy = remote(esum, esum_got, es, er, (nxt, me))
    rate_copy = remote(rate_e, rate_e_got, rs, rr, (prv, me))

    barrier = pltpu.get_barrier_semaphore()

    @pl.when(odd)
    def _():
        signal(barrier, (mirror, me))
        signal(barrier, (prv, me))

        @pl.when(jnp.logical_not(last))
        def _():
            signal(barrier, (nxt, me))

        each_peer(1, lambda p: signal(barrier, (section, lax.rem(me + p, width))))

    load_held = pltpu.make_async_copy(held.at[0], hs, load_h)
    load_act = pltpu.make_async_copy(act.at[0], xs, load_x)
    load_grad = pltpu.make_async_copy(grad.at[0], gs, load_g)
    load_park = pltpu.make_async_copy(park, flags, load_p)
    load_gains = [
        pltpu.make_async_copy(src, dst, load_w.at[i])
        for i, (src, dst) in enumerate(((gq_in, gq), (gk_in, gk), (gv_in, gv)))
    ]
    load_held.start()
    load_act.start()
    load_grad.start()
    for copy in load_gains:
        copy.start()
    load_park.start()

    def squares(ref):
        def step(h, acc):
            v = ref[:, cols(h)].astype(F32)
            return acc + v * v

        return row_sums(lax.fori_loop(0, heads, step, jnp.zeros((SEQ, HD), F32)))

    load_held.wait()
    b0, b1 = squares(hs)
    hsum[0:1] = b0
    hsum[1:2] = b1

    def start_acts():
        @pl.when(act_first)
        def _():
            each_head(lambda h: act_copy(h).start())

    def start_some(h, c):
        held_copy(h).start()
        return c

    @pl.when(even)
    def _():
        pl.semaphore_wait(barrier, jnp.where(first, 2, 3))
        signal(hello, (mirror, me))
        signal(hello, (nxt, me))

        @pl.when(jnp.logical_not(first))
        def _():
            signal(hello, (prv, me))

        hsum_copy.start()
        lax.fori_loop(0, min(FIRST, heads), start_some, 0)
        pl.semaphore_wait(near, 1)
        lax.fori_loop(min(FIRST, heads), heads, start_some, 0)
        start_acts()

    @pl.when(odd)
    def _():
        pl.semaphore_wait(hello, jnp.where(last, 2, 3))
        hsum_copy.start()
        signal(near, (prv, me))
        lax.fori_loop(0, heads, start_some, 0)
        start_acts()

    load_act.wait()
    a0, a1 = squares(xs)
    for copy in load_gains:
        copy.wait()
    load_park.wait()
    flag = flags[mirror]

    @pl.when(even)
    def _():
        esum[0:1] = a0
        esum[1:2] = a1
        hsum_copy.wait_recv()
        esum[2:4] = hsum_got[...]
        esum_copy.start()
        rate_copy.wait_recv()

    @pl.when(odd)
    def _():
        pl.semaphore_wait(barrier, width - 1)
        msg1[0:1] = a0
        msg1[1:2] = a1
        hsum_copy.wait_recv()
        msg1[2:4] = hsum_got[...]
        esum_copy.wait_recv()
        msg1[4:8] = esum_got[...]
        each_peer(1, lambda p: sum_copy(msg1, gat1, s1, r1, p).start())
        gat1[pl.ds(me, 1)] = msg1[...][None]
        each_peer(1, lambda p: sum_copy(msg1, gat1, s1, r1, p).wait_recv())
        rates = lax.rsqrt(jnp.sum(gat1[...], axis=0) / features + EPS)
        rate_e[...] = rates[4:8]
        rate_copy.start()
        rate_e_got[...] = rates[0:4]

    rates = rate_e_got[...]
    rate_f[pl.ds(0, 128)] = as_column(rates[0:1])
    rate_f[pl.ds(128, 128)] = as_column(rates[1:2])
    rate_s[pl.ds(0, 128)] = as_column(rates[2:3])
    rate_s[pl.ds(128, 128)] = as_column(rates[3:4])

    def project(xf, rate, h):
        normed = xf * rate
        return (
            (normed * gq[:, cols(h)]).astype(BF16),
            (normed * gk[:, cols(h)]).astype(BF16),
            (normed * gv[:, cols(h)]).astype(BF16),
        )

    tacc[...] = jnp.zeros((SEQ, HD), F32)

    def backward(h):
        held_copy(h).wait_recv()

        xf = ss[h].astype(F32)
        rate = rate_s[...]
        q, k, v = project(xf, rate, h)
        g = gs[:, cols(h)]
        p0 = softmax_rows(nt(q[0:128], k[0:128]), 0)
        p1 = softmax_rows(nt(q[128:256], k), 128)
        d0 = nt(g[0:128], v[0:128])
        d1 = nt(g[128:256], v)

        def dscore(probs, dprob):
            delta = jnp.sum(probs * dprob, axis=-1, keepdims=True)
            return (probs * (dprob - delta) * SCALE).astype(BF16)

        e0 = dscore(p0, d0)
        e1 = dscore(p1, d1)
        dval = tn(p1.astype(BF16), g[128:256])
        dkey = tn(e1, q[128:256])
        dval0 = dval[0:128] + tn(p0.astype(BF16), g[0:128])
        dkey0 = dkey[0:128] + tn(e0, q[0:128])
        g_q, g_k, g_v = gq[:, cols(h)], gk[:, cols(h)], gv[:, cols(h)]
        dn0 = nn(e0, k[0:128]) * g_q + dkey0 * g_k + dval0 * g_v
        dn1 = nn(e1, k) * g_q + dkey[128:256] * g_k + dval[128:256] * g_v
        zs[h, pl.ds(0, 128)] = g[0:128].astype(F32) + rate[0:128] * dn0
        zs[h, pl.ds(128, 128)] = g[128:256].astype(F32) + rate[128:256] * dn1
        tacc[pl.ds(0, 128)] += dn0 * xf[0:128]
        tacc[pl.ds(128, 128)] += dn1 * xf[128:256]

    @pl.when(act_mid)
    def _():
        each_head(lambda h: act_copy(h).start())

    load_grad.wait()
    each_head(backward)

    t0, t1 = row_sums(tacc[...])
    msg3[0:1] = t0
    msg3[1:2] = t1
    each_peer(1, lambda p: total_copy(p).start())
    gat3[pl.ds(me, 1)] = msg3[...][None]

    @pl.when(act_aft)
    def _():
        each_head(lambda h: act_copy(h).start())

    def forward(h):
        xf = xs[:, cols(h)].astype(F32)
        q, k, v = project(xf, rate_f[...], h)
        p0 = softmax_rows(nt(q[0:128], k[0:128]), 0).astype(BF16)
        p1 = softmax_rows(nt(q[128:256], k), 128).astype(BF16)
        ys[h, pl.ds(0, 128)] = (xf[0:128] + nn(p0, v[0:128])).astype(BF16)
        ys[h, pl.ds(128, 128)] = (xf[128:256] + nn(p1, v)).astype(BF16)

        @pl.when(jnp.logical_not(last))
        def _():
            y_copy(h).start()

    each_head(forward)

    @pl.when(act_later)
    def _():
        each_head(lambda h: act_copy(h).start())

    def zero_grad(h):
        return pltpu.make_async_copy(xn.at[h], grad_out.at[0, :, cols(h)], zero_sem.at[h])

    def held_place(h):
        return pltpu.make_async_copy(ho.at[h], held_out.at[0, :, cols(h)], ho_sem.at[h])

    each_peer(1, lambda p: total_copy(p).wait_recv())
    totals = jnp.sum(gat3[...], axis=0) / features
    rate_f[pl.ds(0, 128)] = as_column(totals[0:1])
    rate_f[pl.ds(128, 128)] = as_column(totals[1:2])
    rate = rate_s[...]
    rate_f[...] = rate_f[...] * (rate * rate * rate)

    def finish(h):
        bo[h] = (zs[h] - ss[h].astype(F32) * rate_f[...]).astype(BF16)

        @pl.when(jnp.logical_not(first))
        def _():
            b_copy(h).start()

    each_head(finish)

    @pl.when(last)
    def _():
        def zero(h):
            xn[h] = jnp.zeros((SEQ, HD), BF16)
            zero_grad(h).start()

        each_head(zero)

    def zero_place(h):
        return pltpu.make_async_copy(xn.at[h], act_out.at[0, :, cols(h)], zero_sem.at[h])

    @pl.when(first)
    def _():
        def zero(h):
            xn[h] = jnp.zeros((SEQ, HD), BF16)
            zero_place(h).start()

        each_head(zero)

    def place(h):
        @pl.when(jnp.logical_not(low))
        def _():
            act_copy(h).wait_recv()

        mine = hs[:, cols(h)]

        @pl.when(low)
        def _():
            ho[h] = mine

        @pl.when(jnp.logical_not(low))
        def _():
            ho[h] = jnp.where(flag == 1, far[h], mine)

        held_place(h).start()

    each_head(place)

    def drain(h):
        held_place(h).wait()
        held_copy(h).wait_send()

        @pl.when(first)
        def _():
            zero_place(h).wait()

        @pl.when(last)
        def _():
            zero_grad(h).wait()

        @pl.when(low)
        def _():
            act_copy(h).wait_send()

        @pl.when(jnp.logical_not(last))
        def _():
            y_copy(h).wait_send()
            b_copy(h).wait_recv()

        @pl.when(jnp.logical_not(first))
        def _():
            y_copy(h).wait_recv()
            b_copy(h).wait_send()

    each_head(drain)

    each_peer(1, lambda p: total_copy(p).wait_send())

    hsum_copy.wait_send()

    @pl.when(even)
    def _():
        esum_copy.wait_send()

    @pl.when(odd)
    def _():
        each_peer(1, lambda p: sum_copy(msg1, gat1, s1, r1, p).wait_send())
        rate_copy.wait_send()


def place_kernel(a, b, c, a_out, b_out, c_out, a_mid, b_mid, c_mid, sems):
    stages = ((a, a_mid, a_out), (b, b_mid, b_out), (c, c_mid, c_out))
    into = [pltpu.make_async_copy(src, mid, sems.at[0, i]) for i, (src, mid, _) in enumerate(stages)]
    outof = [pltpu.make_async_copy(mid, dst, sems.at[1, i]) for i, (_, mid, dst) in enumerate(stages)]
    for copy in into:
        copy.start()
    for first, second in zip(into, outof):
        first.wait()
        second.start()
    for copy in outof:
        copy.wait()


def solution(mesh):
    sections, width = mesh.shape["pipe"], mesh.shape["tp"]

    def shards(act_in, grad_in, held, park, gain_q, gain_k, gain_v):
        heads = act_in.shape[2] // HD
        block = jax.ShapeDtypeStruct(act_in.shape, BF16)
        hbm = pl.BlockSpec(memory_space=pltpu.HBM)
        dma = pltpu.SemaphoreType.DMA

        def body(*refs):
            kernel(heads, sections, width, *refs)

        per_head = [dma((heads,)), dma((heads,))]
        per_peer = [dma((width,)), dma((width,))]
        field = pltpu.VMEM((SEQ, HD), F32)
        rows = pltpu.VMEM((4, 128), F32)
        pair = pltpu.VMEM((2, 128), F32)
        gathered = pltpu.VMEM((width, 4, 128), F32)
        flat = pltpu.VMEM((SEQ, heads * HD), BF16)
        stack = pltpu.VMEM((heads, SEQ, HD), BF16)
        wide_stack = pltpu.VMEM((heads, SEQ, HD), F32)
        gain_row = pltpu.VMEM((1, heads * HD), F32)
        outs = pl.pallas_call(
            body,
            out_shape=(block, block, block),
            in_specs=[hbm] * 7,
            out_specs=(hbm, hbm, hbm),
            scratch_shapes=[
                flat, flat, flat, stack, stack, stack,
                wide_stack, stack,
                gain_row, gain_row, gain_row, pltpu.SMEM((sections,), jnp.int32),
                field, field, field,
                pltpu.VMEM((8, 128), F32), pltpu.VMEM((width, 8, 128), F32), rows, gathered,
                pair, pair, rows, rows, rows, rows,
                stack, stack,
                dma, dma, dma, dma, dma((3,)),
                *per_head, *per_head, *per_head, *per_head,
                *per_peer, *per_peer,
                dma, dma, dma, dma, dma, dma,
                dma((heads,)), dma((heads,)),
                pltpu.SemaphoreType.REGULAR, pltpu.SemaphoreType.REGULAR,
            ],
            compiler_params=pltpu.CompilerParams(
                collective_id=0, has_side_effects=True, vmem_limit_bytes=56 * 1024 * 1024
            ),
            name="relay_tick",
        )(act_in, grad_in, held, park, gain_q, gain_k, gain_v)
        return pl.pallas_call(
            place_kernel,
            out_shape=(block, block, block),
            in_specs=[hbm] * 3,
            out_specs=(hbm, hbm, hbm),
            scratch_shapes=[pltpu.VMEM(block.shape, BF16)] * 3 + [dma((2, 3))],
            compiler_params=pltpu.CompilerParams(vmem_limit_bytes=56 * 1024 * 1024),
            name="place",
        )(*outs)

    wide = P("pipe", None, "tp")
    gain = P("pipe", "tp")
    return jax.shard_map(
        shards,
        mesh=mesh,
        in_specs=(wide, wide, wide, P(), gain, gain, gain),
        out_specs=(wide, wide, wide),
        check_vma=False,
    )
```

time: 69.5 us -> 56.9 us (0.82)
  the two profiles are of different devices: /device:TPU:351 before, /device:TPU:57 now
where the time goes in v2:
time: 56.9 us; the launch traced here: 56.8 us
  Pallas kernels  56.1 us (99%)
  between operations  0.64 us (1%)
    pallas_call x1, Pallas kernels, shards(): pl.pallas_call(body, out_shape=(block, block, block), in_specs=[hbm] * 7,...  54.1 us
    pallas_call x1, Pallas kernels, shards(): pl.pallas_call(place_kernel, out_shape=(block, block, block), in_specs=[h...  2.05 us

profile of v2, /device:TPU:57, one launch (start us, length us, event | category | flops | bytes accessed | tf_op | source)
XLA Modules:
  0.0 56.8 jit_solution(6133808685788569099)
XLA Ops:
  0.6 54.1 %relay_tick.1 = (bf16[1,256,768]{2,1,0:T(8,128)(2,1)}, bf16[1,256,768]{2,1,0:T(8,128)(2,1)}, bf16[1,256,768]{2,1,0:T(8,128)(2,1)}) custom-call(bf16[1,256,768]{2,1,0:T(8,128)(2,1)} %refs_0_.1, bf16[1,256,768]{2,1,0:T(8,128)(2,1)} %refs_1_.1, bf16[1,256,768]{2,1,0:T(8,128)(2,1)} %refs_2_.1, s32[32]{0:T(128)} %refs_3_.1, f32[1,768]{1,0:T(1,128)} %refs_4_.1, ...), custom_call_target="tpu_custom_call" | custom-call | tf_op jit(solution)/shard_map/relay_tick/pallas_call | solution.py:455
  54.7 2.1 %place.1 = (bf16[1,256,768]{2,1,0:T(8,128)(2,1)}, bf16[1,256,768]{2,1,0:T(8,128)(2,1)}, bf16[1,256,768]{2,1,0:T(8,128)(2,1)}) custom-call(bf16[1,256,768]{2,1,0:T(8,128)(2,1)} %get-tuple-element.6.a, bf16[1,256,768]{2,1,0:T(8,128)(2,1)} %get-tuple-element.7.b, bf16[1,256,768]{2,1,0:T(8,128)(2,1)} %get-tuple-element.8.c), custom_call_target="tpu_custom_call" | custom-call | tf_op jit(solution)/shard_map/place/pallas_call | solution.py:480

commit v3 on v2

--- a/solution.py
+++ b/solution.py
@@ -55,7 +55,7 @@
     act_out, grad_out, held_out,
     xs, gs, hs, ss, ys, xn, zs, far, gq, gk, gv, flags,
     rate_f, rate_s, tacc,
-    msg1, gat1, msg3, gat3, hsum, hsum_got, esum, esum_got, rate_e, rate_e_got, bo, ho,
+    msg1, gat1, msg3, gat3, msg4, gat4, hsum, hsum_got, esum, esum_got, rate_e, rate_e_got, bo, ho,
     load_x, load_g, load_h, load_p, load_w,
     held_send, held_recv, y_send, y_recv, b_send, b_recv, far_send, far_recv,
     s1, r1, s3, r3, hs_send, hs_recv, es, er, rs, rr, ho_sem, zero_sem,
@@ -76,9 +76,9 @@
     inner = jnp.logical_and(section >= half // 4, section < half - half // 4)
     depth = lax.rem(me, 4)
     act_first = jnp.logical_and(low, jnp.logical_not(inner))
-    act_mid = jnp.logical_and(inner, depth < 1)
-    act_aft = jnp.logical_and(inner, jnp.logical_and(depth >= 1, depth < 1))
-    act_later = jnp.logical_and(inner, jnp.logical_and(depth >= 1, depth >= 1))
+    act_mid = jnp.logical_and(inner, depth < 2)
+    act_aft = jnp.logical_and(inner, jnp.logical_and(depth >= 2, depth < 2))
+    act_later = jnp.logical_and(inner, jnp.logical_and(depth >= 2, depth >= 2))
 
     def cols(h):
         return pl.ds(pl.multiple_of(h * HD, HD), HD)
@@ -121,8 +121,13 @@
     def sum_copy(msg, gat, send, recv, p):
         return remote(msg, gat.at[me], send.at[p], recv.at[p], (section, lax.rem(me + p, width)))
 
-    def total_copy(p):
-        return remote(msg3, gat3.at[me], s3.at[p], r3.at[p], (section, lax.rem(me + p, width)))
+    row, spot = me // 4, lax.rem(me, 4)
+
+    def along_x(p):
+        return remote(msg3, gat3.at[row], s3.at[p], r3.at[p], (section, lax.rem(row + p, 4) * 4 + spot))
+
+    def along_z(p):
+        return remote(msg4, gat4.at[spot], s3.at[p + 4], r3.at[p + 4], (section, row * 4 + lax.rem(spot + p, 4)))
 
     hsum_copy = remote(hsum, hsum_got, hs_send, hs_recv, (mirror, me))
     esum_copy = remote(esum, esum_got, es, er, (nxt, me))
@@ -290,9 +295,9 @@
     t0, t1 = row_sums(tacc[...])
     msg3[0:1] = t0
     msg3[1:2] = t1
-    each_peer(1, lambda p: total_copy(p).start())
-    gat3[pl.ds(me, 1)] = msg3[...][None]
-
+    for p in range(1, 4):
+        along_x(p).start()
+    gat3[pl.ds(row, 1)] = msg3[...][None]
     @pl.when(act_aft)
     def _():
         each_head(lambda h: act_copy(h).start())
@@ -309,7 +314,17 @@
         def _():
             y_copy(h).start()
 
-    each_head(forward)
+    lax.fori_loop(0, 3, lambda h, c: (forward(h), c)[1], 0)
+
+    for p in range(1, 4):
+        along_x(p).wait_recv()
+    mid = jnp.sum(gat3[...], axis=0)
+    msg4[...] = mid
+    for p in range(1, 4):
+        along_z(p).start()
+    gat4[pl.ds(spot, 1)] = mid[None]
+
+    lax.fori_loop(3, heads, lambda h, c: (forward(h), c)[1], 0)
 
     @pl.when(act_later)
     def _():
@@ -321,8 +336,9 @@
     def held_place(h):
         return pltpu.make_async_copy(ho.at[h], held_out.at[0, :, cols(h)], ho_sem.at[h])
 
-    each_peer(1, lambda p: total_copy(p).wait_recv())
-    totals = jnp.sum(gat3[...], axis=0) / features
+    for p in range(1, 4):
+        along_z(p).wait_recv()
+    totals = jnp.sum(gat4[...], axis=0) / features
     rate_f[pl.ds(0, 128)] = as_column(totals[0:1])
     rate_f[pl.ds(128, 128)] = as_column(totals[1:2])
     rate = rate_s[...]
@@ -403,7 +419,9 @@
 
     each_head(drain)
 
-    each_peer(1, lambda p: total_copy(p).wait_send())
+    for p in range(1, 4):
+        along_x(p).wait_send()
+        along_z(p).wait_send()
 
     hsum_copy.wait_send()
 
@@ -447,7 +465,7 @@
         field = pltpu.VMEM((SEQ, HD), F32)
         rows = pltpu.VMEM((4, 128), F32)
         pair = pltpu.VMEM((2, 128), F32)
-        gathered = pltpu.VMEM((width, 4, 128), F32)
+        four = pltpu.VMEM((4, 2, 128), F32)
         flat = pltpu.VMEM((SEQ, heads * HD), BF16)
         stack = pltpu.VMEM((heads, SEQ, HD), BF16)
         wide_stack = pltpu.VMEM((heads, SEQ, HD), F32)
@@ -462,7 +480,7 @@
                 wide_stack, stack,
                 gain_row, gain_row, gain_row, pltpu.SMEM((sections,), jnp.int32),
                 field, field, field,
-                pltpu.VMEM((8, 128), F32), pltpu.VMEM((width, 8, 128), F32), rows, gathered,
+                pltpu.VMEM((8, 128), F32), pltpu.VMEM((width, 8, 128), F32), pair, four, pair, four,
                 pair, pair, rows, rows, rows, rows,
                 stack, stack,
                 dma, dma, dma, dma, dma((3,)),

time: 56.9 us -> 53.8 us (0.946)
  the two profiles are of different devices: /device:TPU:57 before, /device:TPU:1 now
where the time goes in v3:
time: 53.8 us; the launch traced here: 52.9 us
  Pallas kernels  52.3 us (97%)
  between operations  0.64 us (1%)
    pallas_call x1, Pallas kernels, shards(): pl.pallas_call(body, out_shape=(block, block, block), in_specs=[hbm] * 7,...  50.3 us
    pallas_call x1, Pallas kernels, shards(): pl.pallas_call(place_kernel, out_shape=(block, block, block), in_specs=[h...  2.05 us

profile of v3, /device:TPU:1, one launch (start us, length us, event | category | flops | bytes accessed | tf_op | source)
XLA Modules:
  0.0 52.9 jit_solution(7063612579923191050)
XLA Ops:
  0.6 50.3 %relay_tick.1 = (bf16[1,256,768]{2,1,0:T(8,128)(2,1)}, bf16[1,256,768]{2,1,0:T(8,128)(2,1)}, bf16[1,256,768]{2,1,0:T(8,128)(2,1)}) custom-call(bf16[1,256,768]{2,1,0:T(8,128)(2,1)} %refs_0_.1, bf16[1,256,768]{2,1,0:T(8,128)(2,1)} %refs_1_.1, bf16[1,256,768]{2,1,0:T(8,128)(2,1)} %refs_2_.1, s32[32]{0:T(128)} %refs_3_.1, f32[1,768]{1,0:T(1,128)} %refs_4_.1, ...), custom_call_target="tpu_custom_call" | custom-call | tf_op jit(solution)/shard_map/relay_tick/pallas_call | solution.py:473
  50.9 2.1 %place.1 = (bf16[1,256,768]{2,1,0:T(8,128)(2,1)}, bf16[1,256,768]{2,1,0:T(8,128)(2,1)}, bf16[1,256,768]{2,1,0:T(8,128)(2,1)}) custom-call(bf16[1,256,768]{2,1,0:T(8,128)(2,1)} %get-tuple-element.6.a, bf16[1,256,768]{2,1,0:T(8,128)(2,1)} %get-tuple-element.7.b, bf16[1,256,768]{2,1,0:T(8,128)(2,1)} %get-tuple-element.8.c), custom_call_target="tpu_custom_call" | custom-call | tf_op jit(solution)/shard_map/place/pallas_call | solution.py:498

commit v4 on v3

--- a/solution.py
+++ b/solution.py
@@ -12,7 +12,8 @@
 F32 = jnp.float32
 BF16 = jnp.bfloat16
 SCALE = HD ** (-0.5)
-FIRST = 2
+FIRST_MIDDLE = 1
+FIRST_BEHIND = 4
 
 
 def nt(a, b):
@@ -75,10 +76,11 @@
     low = section < half
     inner = jnp.logical_and(section >= half // 4, section < half - half // 4)
     depth = lax.rem(me, 4)
+    eighth = lax.rem(section // (sections // 8), 4)
+    at_middle = jnp.logical_or(eighth == 0, eighth == 3)
     act_first = jnp.logical_and(low, jnp.logical_not(inner))
     act_mid = jnp.logical_and(inner, depth < 2)
-    act_aft = jnp.logical_and(inner, jnp.logical_and(depth >= 2, depth < 2))
-    act_later = jnp.logical_and(inner, jnp.logical_and(depth >= 2, depth >= 2))
+    act_later = jnp.logical_and(inner, depth >= 2)
 
     def cols(h):
         return pl.ds(pl.multiple_of(h * HD, HD), HD)
@@ -193,9 +195,10 @@
             signal(hello, (prv, me))
 
         hsum_copy.start()
-        lax.fori_loop(0, min(FIRST, heads), start_some, 0)
+        some = jnp.where(at_middle, FIRST_MIDDLE, FIRST_BEHIND)
+        lax.fori_loop(0, some, start_some, 0)
         pl.semaphore_wait(near, 1)
-        lax.fori_loop(min(FIRST, heads), heads, start_some, 0)
+        lax.fori_loop(some, heads, start_some, 0)
         start_acts()
 
     @pl.when(odd)
@@ -298,10 +301,6 @@
     for p in range(1, 4):
         along_x(p).start()
     gat3[pl.ds(row, 1)] = msg3[...][None]
-    @pl.when(act_aft)
-    def _():
-        each_head(lambda h: act_copy(h).start())
-
     def forward(h):
         xf = xs[:, cols(h)].astype(F32)
         q, k, v = project(xf, rate_f[...], h)
@@ -310,7 +309,7 @@
         ys[h, pl.ds(0, 128)] = (xf[0:128] + nn(p0, v[0:128])).astype(BF16)
         ys[h, pl.ds(128, 128)] = (xf[128:256] + nn(p1, v)).astype(BF16)
 
-        @pl.when(jnp.logical_not(last))
+        @pl.when(jnp.logical_and(jnp.logical_not(last), h >= 3))
         def _():
             y_copy(h).start()
 
@@ -323,6 +322,10 @@
     for p in range(1, 4):
         along_z(p).start()
     gat4[pl.ds(spot, 1)] = mid[None]
+
+    @pl.when(jnp.logical_not(last))
+    def _():
+        lax.fori_loop(0, min(3, heads), lambda h, c: (y_copy(h).start(), c)[1], 0)
 
     lax.fori_loop(3, heads, lambda h, c: (forward(h), c)[1], 0)
 

time: 53.8 us -> 53.2 us (0.989); the launches traced: 52.9 us -> 53 us
  no operation moved by 1% of the time
where the time goes in v4:
time: 53.2 us; the launch traced here: 53 us
  Pallas kernels  52.4 us (98%)
  between operations  0.64 us (1%)
    pallas_call x1, Pallas kernels, shards(): pl.pallas_call(body, out_shape=(block, block, block), in_specs=[hbm] * 7,...  50.3 us
    pallas_call x1, Pallas kernels, shards(): pl.pallas_call(place_kernel, out_shape=(block, block, block), in_specs=[h...  2.05 us

profile of v4, /device:TPU:1, one launch (start us, length us, event | category | flops | bytes accessed | tf_op | source)
XLA Modules:
  0.0 53.0 jit_solution(1823854034298491706)
XLA Ops:
  0.6 50.3 %relay_tick.1 = (bf16[1,256,768]{2,1,0:T(8,128)(2,1)}, bf16[1,256,768]{2,1,0:T(8,128)(2,1)}, bf16[1,256,768]{2,1,0:T(8,128)(2,1)}) custom-call(bf16[1,256,768]{2,1,0:T(8,128)(2,1)} %refs_0_.1, bf16[1,256,768]{2,1,0:T(8,128)(2,1)} %refs_1_.1, bf16[1,256,768]{2,1,0:T(8,128)(2,1)} %refs_2_.1, s32[32]{0:T(128)} %refs_3_.1, f32[1,768]{1,0:T(1,128)} %refs_4_.1, ...), custom_call_target="tpu_custom_call" | custom-call | tf_op jit(solution)/shard_map/relay_tick/pallas_call | solution.py:476
  51.0 2.1 %place.1 = (bf16[1,256,768]{2,1,0:T(8,128)(2,1)}, bf16[1,256,768]{2,1,0:T(8,128)(2,1)}, bf16[1,256,768]{2,1,0:T(8,128)(2,1)}) custom-call(bf16[1,256,768]{2,1,0:T(8,128)(2,1)} %get-tuple-element.6.a, bf16[1,256,768]{2,1,0:T(8,128)(2,1)} %get-tuple-element.7.b, bf16[1,256,768]{2,1,0:T(8,128)(2,1)} %get-tuple-element.8.c), custom_call_target="tpu_custom_call" | custom-call | tf_op jit(solution)/shard_map/place/pallas_call | solution.py:501

commit v5 on v4

--- a/solution.py
+++ b/solution.py
@@ -13,7 +13,7 @@
 BF16 = jnp.bfloat16
 SCALE = HD ** (-0.5)
 FIRST_MIDDLE = 1
-FIRST_BEHIND = 4
+FIRST_BEHIND = 3
 
 
 def nt(a, b):

time: 53.2 us -> 53.2 us (level)
  no operation moved by 1% of the time
where the time goes in v5:
time: 53.2 us; the launch traced here: 53 us
  Pallas kernels  52.4 us (98%)
  between operations  0.64 us (1%)
    pallas_call x1, Pallas kernels, shards(): pl.pallas_call(body, out_shape=(block, block, block), in_specs=[hbm] * 7,...  50.3 us
    pallas_call x1, Pallas kernels, shards(): pl.pallas_call(place_kernel, out_shape=(block, block, block), in_specs=[h...  2.05 us

profile of v5, /device:TPU:1, one launch (start us, length us, event | category | flops | bytes accessed | tf_op | source)
XLA Modules:
  0.0 53.0 jit_solution(15609475953233594092)
XLA Ops:
  0.6 50.3 %relay_tick.1 = (bf16[1,256,768]{2,1,0:T(8,128)(2,1)}, bf16[1,256,768]{2,1,0:T(8,128)(2,1)}, bf16[1,256,768]{2,1,0:T(8,128)(2,1)}) custom-call(bf16[1,256,768]{2,1,0:T(8,128)(2,1)} %refs_0_.1, bf16[1,256,768]{2,1,0:T(8,128)(2,1)} %refs_1_.1, bf16[1,256,768]{2,1,0:T(8,128)(2,1)} %refs_2_.1, s32[32]{0:T(128)} %refs_3_.1, f32[1,768]{1,0:T(1,128)} %refs_4_.1, ...), custom_call_target="tpu_custom_call" | custom-call | tf_op jit(solution)/shard_map/relay_tick/pallas_call | solution.py:476
  51.0 2.1 %place.1 = (bf16[1,256,768]{2,1,0:T(8,128)(2,1)}, bf16[1,256,768]{2,1,0:T(8,128)(2,1)}, bf16[1,256,768]{2,1,0:T(8,128)(2,1)}) custom-call(bf16[1,256,768]{2,1,0:T(8,128)(2,1)} %get-tuple-element.6.a, bf16[1,256,768]{2,1,0:T(8,128)(2,1)} %get-tuple-element.7.b, bf16[1,256,768]{2,1,0:T(8,128)(2,1)} %get-tuple-element.8.c), custom_call_target="tpu_custom_call" | custom-call | tf_op jit(solution)/shard_map/place/pallas_call | solution.py:501

commit v6 on v4

--- a/solution.py
+++ b/solution.py
@@ -309,11 +309,11 @@
         ys[h, pl.ds(0, 128)] = (xf[0:128] + nn(p0, v[0:128])).astype(BF16)
         ys[h, pl.ds(128, 128)] = (xf[128:256] + nn(p1, v)).astype(BF16)
 
-        @pl.when(jnp.logical_and(jnp.logical_not(last), h >= 3))
+        @pl.when(jnp.logical_and(jnp.logical_not(last), h >= 4))
         def _():
             y_copy(h).start()
 
-    lax.fori_loop(0, 3, lambda h, c: (forward(h), c)[1], 0)
+    lax.fori_loop(0, 4, lambda h, c: (forward(h), c)[1], 0)
 
     for p in range(1, 4):
         along_x(p).wait_recv()
@@ -325,9 +325,9 @@
 
     @pl.when(jnp.logical_not(last))
     def _():
-        lax.fori_loop(0, min(3, heads), lambda h, c: (y_copy(h).start(), c)[1], 0)
-
-    lax.fori_loop(3, heads, lambda h, c: (forward(h), c)[1], 0)
+        lax.fori_loop(0, 4, lambda h, c: (y_copy(h).start(), c)[1], 0)
+
+    lax.fori_loop(4, heads, lambda h, c: (forward(h), c)[1], 0)
 
     @pl.when(act_later)
     def _():

time: 53.2 us -> 53.2 us (level)
  no operation moved by 1% of the time
where the time goes in v6:
time: 53.2 us; the launch traced here: 53 us
  Pallas kernels  52.4 us (98%)
  between operations  0.64 us (1%)
    pallas_call x1, Pallas kernels, shards(): pl.pallas_call(body, out_shape=(block, block, block), in_specs=[hbm] * 7,...  50.3 us
    pallas_call x1, Pallas kernels, shards(): pl.pallas_call(place_kernel, out_shape=(block, block, block), in_specs=[h...  2.05 us

profile of v6, /device:TPU:1, one launch (start us, length us, event | category | flops | bytes accessed | tf_op | source)
XLA Modules:
  0.0 53.0 jit_solution(14712691996506605570)
XLA Ops:
  0.6 50.3 %relay_tick.1 = (bf16[1,256,768]{2,1,0:T(8,128)(2,1)}, bf16[1,256,768]{2,1,0:T(8,128)(2,1)}, bf16[1,256,768]{2,1,0:T(8,128)(2,1)}) custom-call(bf16[1,256,768]{2,1,0:T(8,128)(2,1)} %refs_0_.1, bf16[1,256,768]{2,1,0:T(8,128)(2,1)} %refs_1_.1, bf16[1,256,768]{2,1,0:T(8,128)(2,1)} %refs_2_.1, s32[32]{0:T(128)} %refs_3_.1, f32[1,768]{1,0:T(1,128)} %refs_4_.1, ...), custom_call_target="tpu_custom_call" | custom-call | tf_op jit(solution)/shard_map/relay_tick/pallas_call | solution.py:476
  51.0 2.1 %place.1 = (bf16[1,256,768]{2,1,0:T(8,128)(2,1)}, bf16[1,256,768]{2,1,0:T(8,128)(2,1)}, bf16[1,256,768]{2,1,0:T(8,128)(2,1)}) custom-call(bf16[1,256,768]{2,1,0:T(8,128)(2,1)} %get-tuple-element.6.a, bf16[1,256,768]{2,1,0:T(8,128)(2,1)} %get-tuple-element.7.b, bf16[1,256,768]{2,1,0:T(8,128)(2,1)} %get-tuple-element.8.c), custom_call_target="tpu_custom_call" | custom-call | tf_op jit(solution)/shard_map/place/pallas_call | solution.py:501
